TPU v7x, 512 devices: a whole 4x8x8 slice. The times are simulated.
512 devices in a mesh: outer: 128 (over z, y, core), inner: 4 (over x).
Axes of the slice: x: 4, y: 8, z: 8, core: 2. Of those that a mesh axis runs over, the one named last changes fastest.
Arguments:
- query_states: bfloat16 [65536, 4096], P(('outer', 'inner')), may hold values from -6 to 6
- key_states: bfloat16 [65536, 4096], P(('outer', 'inner')), may hold values from -6 to 6
- value_states: bfloat16 [65536, 4096], P(('outer', 'inner')), may hold values from -6 to 6
- doc_lengths: int32 [128], replicated, may hold values from 1 to 1024, 65536 in all
- slopes: float32 [32], replicated, may hold values from 0.00024414062 to 0.0625
Outputs:
- attended: bfloat16 [65536, 4096], P(('outer', 'inner'))
Inputs may be any that keep to these rules, and one draw needn't show every extreme that they name: `doc_lengths`: the lengths add up to 65536; the longest is exactly 1024.
All inputs are finite; a program needn't handle non-finite values.
Results may differ from a plain program's by a relative error of at most 0.0045.
Values may be sent and summed in bfloat16 or wider, within the bound.
No kernel may reach another device: no remote copies, remote signals or barrier semaphores. Data moves between devices by JAX's collectives and lax.ppermute only.
A program may use at most 64 MiB of HBM per device.

v0:
```python
import math
import jax
import jax.numpy as jnp
from jax import lax
from jax.sharding import PartitionSpec as P

SPAN = 2
NEG_FILL = -1e30


def shifted(value, axis, steps):
    count = lax.axis_size(axis)
    first, last = (max(0, -steps), min(count, count - steps))
    return lax.ppermute(value, axis, [(source, source + steps) for source in range(first, last)])


def document_of(positions, doc_lengths):
    boundary = jnp.cumsum(doc_lengths)
    return jnp.sum((boundary[None, :] <= positions[:, None]).astype(jnp.int32), axis=1)


def empty_status(row_count, head_count, head_width):
    return (
        jnp.full((row_count, head_count), NEG_FILL, jnp.float32),
        jnp.zeros((row_count, head_count), jnp.float32),
        jnp.zeros((row_count, head_count, head_width), jnp.float32),
    )


def attend_block(status, query_parts, key_slab, value_slab, key_pos, key_doc, slopes):
    query_rows, query_pos, query_doc = query_parts
    allowed = (query_doc[:, None] == key_doc[None, :]) & (key_pos[None, :] <= query_pos[:, None])

    def update(current):
        running_max, row_total, weighted_sum = current
        scores = jnp.einsum(
            "qhd,khd->qhk", query_rows, key_slab, preferred_element_type=jnp.float32
        )
        scores = scores * (1.0 / math.sqrt(query_rows.shape[-1]))
        distance = (query_pos[:, None] - key_pos[None, :]).astype(jnp.float32)
        scores = scores - slopes[None, :, None] * distance[:, None, :]
        scores = jnp.where(allowed[:, None, :], scores, NEG_FILL)
        new_max = jnp.maximum(running_max, jnp.max(scores, axis=-1))
        weights = jnp.where(allowed[:, None, :], jnp.exp(scores - new_max[:, :, None]), 0.0)
        rescale = jnp.exp(running_max - new_max)
        row_total = row_total * rescale + jnp.sum(weights, axis=-1)
        products = jnp.einsum(
            "qhk,khd->qhd",
            weights.astype(jnp.bfloat16),
            value_slab,
            preferred_element_type=jnp.float32,
        )
        weighted_sum = weighted_sum * rescale[:, :, None] + products
        return (new_max, row_total, weighted_sum)

    def unchanged(current):
        return current

    return lax.cond(jnp.any(allowed), update, unchanged, status)


def attend_keys(status, query_parts, key_slab, value_slab, key_pos, slopes, doc_lengths):
    key_doc = document_of(key_pos, doc_lengths)
    key_count = key_slab.shape[0]
    slab_rows = 256
    pieces = key_count // slab_rows
    stacked = (
        key_slab.reshape((pieces, slab_rows) + key_slab.shape[1:]),
        value_slab.reshape((pieces, slab_rows) + value_slab.shape[1:]),
        key_pos.reshape(pieces, slab_rows),
        key_doc.reshape(pieces, slab_rows),
    )

    def scan_step(current, portion):
        return (
            attend_block(
                current, query_parts, portion[0], portion[1], portion[2], portion[3], slopes
            ),
            None,
        )

    result, unused = lax.scan(scan_step, status, stacked)
    return result


def combine(first_status, second_status):
    new_max = jnp.maximum(first_status[0], second_status[0])
    left_scale = jnp.exp(first_status[0] - new_max)
    right_scale = jnp.exp(second_status[0] - new_max)
    return (
        new_max,
        first_status[1] * left_scale + second_status[1] * right_scale,
        first_status[2] * left_scale[:, :, None] + second_status[2] * right_scale[:, :, None],
    )


def queries_from_later(query_rows, hops_back):
    return shifted(query_rows, "outer", -hops_back)


def partials_home(status, hops_back):
    running_max, row_total, weighted_sum = status
    moved_max, moved_total, moved_sum = shifted(
        (running_max, row_total, weighted_sum), "outer", hops_back
    )
    return (jnp.where(moved_total > 0.0, moved_max, NEG_FILL), moved_total, moved_sum)


def rows_of(status, slot_index, row_count):
    return tuple(
        (member[slot_index * row_count : (slot_index + 1) * row_count] for member in status)
    )


def bring_home(status, row_count, span_count):
    own_status = rows_of(status, 0, row_count)
    distant = [rows_of(status, hops_back, row_count) for hops_back in range(1, span_count + 1)]
    merged = own_status
    for hops_back in range(1, span_count + 1):
        merged = combine(merged, partials_home(distant[hops_back - 1], hops_back))
    return merged


def with_later_queries(own_rows, own_pos, group_rows, span_count, doc_lengths):
    rows_list = [own_rows]
    pos_list = [own_pos]
    for hops_back in range(1, span_count + 1):
        rows_list.append(queries_from_later(own_rows, hops_back))
        pos_list.append(own_pos + hops_back * group_rows)
    all_pos = jnp.concatenate(pos_list)
    return (jnp.concatenate(rows_list, axis=0), all_pos, document_of(all_pos, doc_lengths))


def normalize(status):
    return (status[2] / status[1][:, :, None]).astype(jnp.bfloat16)


def per_device(query_states, key_states, value_states, doc_lengths, slopes):
    rows_dev = query_states.shape[0]
    head_count = slopes.shape[0]
    head_width = query_states.shape[1] // head_count
    inner_count = lax.axis_size("inner")
    group_index = lax.axis_index("outer")
    inner_index = lax.axis_index("inner")
    group_rows = rows_dev * inner_count
    group_start = group_index * group_rows
    own_queries = query_states.reshape(rows_dev, head_count, head_width)
    own_pos = group_start + inner_index * rows_dev + jnp.arange(rows_dev, dtype=jnp.int32)
    query_parts = with_later_queries(own_queries, own_pos, group_rows, SPAN, doc_lengths)
    status = empty_status(query_parts[0].shape[0], head_count, head_width)
    portions = (
        lax.all_gather(
            key_states.reshape(rows_dev, head_count, head_width), "inner", axis=0, tiled=True
        ),
        lax.all_gather(
            value_states.reshape(rows_dev, head_count, head_width), "inner", axis=0, tiled=True
        ),
    )
    key_pos = group_start + jnp.arange(portions[0].shape[0], dtype=jnp.int32)
    status = attend_keys(
        status, query_parts, portions[0], portions[1], key_pos, slopes, doc_lengths
    )
    combined = bring_home(status, rows_dev, SPAN)
    return normalize(combined).reshape(rows_dev, head_count * head_width)


def solution(mesh):
    placed = (
        P(("outer", "inner"), None),
        P(("outer", "inner"), None),
        P(("outer", "inner"), None),
        P(),
        P(),
    )
    return jax.shard_map(
        per_device,
        mesh=mesh,
        in_specs=placed,
        out_specs=P(("outer", "inner"), None),
        check_vma=False,
    )
```

profile of v0, /device:TPU:256, one launch (start us, length us, event | category | flops | bytes accessed | tf_op | source)
XLA Modules:
  0.0 273.0 jit_solution(12478321590578903642)
XLA Ops:
  6.5 2.5 copy.32
  9.1 0.0 all-gather.3.cloned.1.call-update
  9.1 0.0 all-gather.5.cloned.1.call-start
  9.1 2.4 copy.33
  11.6 0.0 all-gather.5.cloned.1.call-update
  11.6 0.7 copy.25
  12.3 3.9 %collective-permute-start = (bf16[128,32,128]{0,2,1:T(8,128)(2,1)S(1)}, bf16[128,32,128]{0,2,1:T(8,128)(2,1)S(1)}, u32[]{:S(2)}, u32[]{:S(2)}) collective-permute-start(bf16[128,32,128]{0,2,1:T(8,128)(2,1)S(1)} %bitcast.49), channel_id=1, source_target_pairs={{4,0},{8,4},{12,8},{16,12},{20,16},{24,20},{28,24},{32,28},{36,32}... | collective-permute-start | bytes 3145736 | tf_op jit(solution)/shard_map/ppermute | solution.py:14
  16.2 3.3 %collective-permute-start.1 = (bf16[128,32,128]{0,2,1:T(8,128)(2,1)S(1)}, bf16[128,32,128]{0,2,1:T(8,128)(2,1)}, u32[]{:S(2)}, u32[]{:S(2)}) collective-permute-start(bf16[128,32,128]{0,2,1:T(8,128)(2,1)S(1)} %bitcast.50), channel_id=1, source_target_pairs={{8,0},{12,4},{16,8},{20,12},{24,16},{28,20},{32,24},{36,28},{40,32... | collective-permute-start | bytes 3145736 | tf_op jit(solution)/shard_map/ppermute | solution.py:14
  19.5 0.1 copy.24
  19.6 0.2 reduce-window.8
  19.8 0.1 reduce
  19.9 0.2 convert_reduce_fusion
  20.2 0.2 convert_reduce_fusion.1
  20.4 17.2 %collective-permute-done = bf16[128,32,128]{0,2,1:T(8,128)(2,1)S(1)} collective-permute-done((bf16[128,32,128]{0,2,1:T(8,128)(2,1)S(1)}, bf16[128,32,128]{0,2,1:T(8,128)(2,1)S(1)}, u32[]{:S(2)}, u32[]{:S(2)}) %collective-permute-start) | collective-permute-done | bytes 1048608 | tf_op jit(solution)/shard_map/ppermute | solution.py:14
  37.6 1.0 copy-done.4
  38.7 12.4 %collective-permute-done.1 = bf16[128,32,128]{0,2,1:T(8,128)(2,1)} collective-permute-done((bf16[128,32,128]{0,2,1:T(8,128)(2,1)S(1)}, bf16[128,32,128]{0,2,1:T(8,128)(2,1)}, u32[]{:S(2)}, u32[]{:S(2)}) %collective-permute-start.1) | collective-permute-done | bytes 1048608 | tf_op jit(solution)/shard_map/ppermute | solution.py:14
  51.1 2.4 pad_maximum_fusion
  53.5 2.9 %copy.27 = bf16[384,32,128]{2,0,1:T(8,128)(2,1)} copy(bf16[384,32,128]{0,2,1:T(8,128)(2,1)S(1)} %pad_maximum_fusion) | data formatting | bytes 6291456 | tf_op jit(solution)/shard_map/while | solution.py:82
  56.4 8.4 %all-gather.3.cloned.1.call-done = bf16[512,32,128]{2,1,0:T(8,128)(2,1)} async-done(((bf16[128,32,128]{2,1,0:T(8,128)(2,1)}), bf16[512,32,128]{2,1,0:T(8,128)(2,1)}) %all-gather.3.cloned.1.call-update) | async-done | bytes 4194320 | tf_op jit(solution)/shard_map/all_gather | solution.py:152
  64.8 5.8 %copy.26 = bf16[2,256,32,128]{3,1,2,0:T(8,128)(2,1)} copy(bf16[2,256,32,128]{3,2,1,0:T(8,128)(2,1)} %bitcast.45) | data formatting | bytes 8388608 | tf_op jit(solution)/shard_map/while | solution.py:82
  70.7 50.3 %all-gather.5.cloned.1.call-done = bf16[512,32,128]{2,1,0:T(8,128)(2,1)} async-done(((bf16[128,32,128]{2,1,0:T(8,128)(2,1)}), bf16[512,32,128]{2,1,0:T(8,128)(2,1)}) %all-gather.5.cloned.1.call-update) | async-done | bytes 4194320 | tf_op jit(solution)/shard_map/all_gather | solution.py:155
  121.0 6.0 %copy.28 = bf16[2,256,32,128]{3,1,2,0:T(8,128)(2,1)} copy(bf16[2,256,32,128]{3,2,1,0:T(8,128)(2,1)} %bitcast.46) | data formatting | bytes 8388608 | tf_op jit(solution)/shard_map/while | solution.py:82
  127.0 3.4 %broadcast_in_dim.61 = f32[384,32,128]{2,0,1:T(8,128)} broadcast(f32[]{:T(128)} %constant.59.clone.1), dimensions={} | broadcast | bytes 6291460 | tf_op jit(solution)/shard_map/broadcast_in_dim | solution.py:26
  130.4 41.3 %while.14 = (s32[]{:T(128)}, f32[384,32]{0,1:T(8,128)S(1)}, f32[384,32]{0,1:T(8,128)S(1)}, f32[384,32,128]{2,0,1:T(8,128)}, s32[384]{0:T(512)S(1)}, /*index=5*/s...) while((s32[]{:T(128)}, f32[384,32]{0,1:T(8,128)S(1)}, ...), condition=%wide.region_9.10_spmd, body=%wide.region_3.9_spmd.sunk | while | flops 1674141696 | bytes 104477920 | solution.py:82
  130.4 0.8 fusion.31
  131.9 19.2 %conditional.2 = ((f32[384,32]{0,1:T(8,128)S(1)}, f32[384,32]{0,1:T(8,128)S(1)}, f32[384,32,128]{2,0,1:T(8,128)})) conditional(s32[]{:T(128)} %convert_element_type.41, (f32[384,32]{0,1:T(8,128)S(1)}, f32[384,32]{0,1:T(8,128)S(1)}, f32[384,32,128]{2,0,1:T(8,128)}) %tuple.50, (pred[384,256]{0,1:T(8,128)(4,1)S(1)}, bf16[2,256,32,128]{3,1,2,0:T(8,128)(2,1)}, ...), branch_computations={%region_5.5_spmd, %region_6.8_spmd} | conditional | flops 1673748480 | bytes 104370152 | solution.py:59
  131.9 0.1 subtract_convert_fusion
  132.0 4.5 %fusion.3 = (f32[384,32]{0,1:T(8,128)S(1)}, f32[32,256,384]{2,1,0:T(8,128)S(1)}) fusion(f32[384,256]{0,1:T(8,128)S(1)} %subtract_convert_fusion, f32[32]{0:T(128)S(1)} %get-tuple-element.141, pred[384,256]{0,1:T(8,128)(4,1)S(1)} %get-tuple-element.137, bf16[384,32,128]{2,0,1:T(8,128)(2,1)S(1)} %get-tuple-element.140, ...), kind=kOutput, calls=%fused_computation.5 | convolution fusion | flops 821022720 | bytes 18367104 | tf_op jit(solution)/shard_map/while/body/eval_jaxpr/cond/branch_1_fun/qhd,khd->qhk/dot_general | solution.py:36
  136.6 4.3 %fusion.2 = f32[384,32]{0,1:T(8,128)S(1)} fusion(f32[32,256,384]{2,1,0:T(8,128)S(1)} %get-tuple-element.239, f32[384,32]{0,1:T(8,128)S(1)} %max.8, f32[384,256]{0,1:T(8,128)S(1)} %subtract_convert_fusion, f32[32]{0:T(128)S(1)} %get-tuple-element.141, pred[384,256]{0,1:T(8,128)(4,1)S(1)} %get-tuple-element.137), kind=kLoop, calls=%fused_computation.4 | loop fusion | flops 22007808 | bytes 13172864 | tf_op jit(solution)/shard_map/while/body/eval_jaxpr/cond/branch_1_fun/reduce_sum | solution.py:46
  140.9 7.5 %bitcast_add_fusion = f32[384,32,128]{2,0,1:T(8,128)S(1)} fusion(f32[384,32,128]{2,0,1:T(8,128)S(1)} %bitcast.44, f32[384,32]{0,1:T(8,128)S(1)} %get-tuple-element.230, f32[32,256,384]{2,1,0:T(8,128)S(1)} %get-tuple-element.239, f32[384,32]{0,1:T(8,128)S(1)} %max.8, f32[384,256]{0,1:T(8,128)S(1)} %subtract_convert_fusion, f32[32]{0:T(128)S(1)} %get-tuple-element.141, ...), kind=kOutput, calls=%fused_computation.6 | convolution fusion | flops 830472192 | bytes 27853440 | tf_op jit(solution)/shard_map/while/body/eval_jaxpr/cond/branch_1_fun/qhk,khd->qhd/dot_general | solution.py:47
  148.4 2.7 copy-done
  151.1 0.8 fusion.31
  152.5 19.2 %conditional.2 = ((f32[384,32]{0,1:T(8,128)S(1)}, f32[384,32]{0,1:T(8,128)S(1)}, f32[384,32,128]{2,0,1:T(8,128)})) conditional(s32[]{:T(128)} %convert_element_type.41, (f32[384,32]{0,1:T(8,128)S(1)}, f32[384,32]{0,1:T(8,128)S(1)}, f32[384,32,128]{2,0,1:T(8,128)}) %tuple.50, (pred[384,256]{0,1:T(8,128)(4,1)S(1)}, bf16[2,256,32,128]{3,1,2,0:T(8,128)(2,1)}, ...), branch_computations={%region_5.5_spmd, %region_6.8_spmd} | conditional | flops 1673748480 | bytes 104370152 | solution.py:59
  152.5 0.1 subtract_convert_fusion
  152.7 4.5 %fusion.3 = (f32[384,32]{0,1:T(8,128)S(1)}, f32[32,256,384]{2,1,0:T(8,128)S(1)}) fusion(f32[384,256]{0,1:T(8,128)S(1)} %subtract_convert_fusion, f32[32]{0:T(128)S(1)} %get-tuple-element.141, pred[384,256]{0,1:T(8,128)(4,1)S(1)} %get-tuple-element.137, bf16[384,32,128]{2,0,1:T(8,128)(2,1)S(1)} %get-tuple-element.140, ...), kind=kOutput, calls=%fused_computation.5 | convolution fusion | flops 821022720 | bytes 18367104 | tf_op jit(solution)/shard_map/while/body/eval_jaxpr/cond/branch_1_fun/qhd,khd->qhk/dot_general | solution.py:36
  157.2 4.3 %fusion.2 = f32[384,32]{0,1:T(8,128)S(1)} fusion(f32[32,256,384]{2,1,0:T(8,128)S(1)} %get-tuple-element.239, f32[384,32]{0,1:T(8,128)S(1)} %max.8, f32[384,256]{0,1:T(8,128)S(1)} %subtract_convert_fusion, f32[32]{0:T(128)S(1)} %get-tuple-element.141, pred[384,256]{0,1:T(8,128)(4,1)S(1)} %get-tuple-element.137), kind=kLoop, calls=%fused_computation.4 | loop fusion | flops 22007808 | bytes 13172864 | tf_op jit(solution)/shard_map/while/body/eval_jaxpr/cond/branch_1_fun/reduce_sum | solution.py:46
  161.6 7.5 %bitcast_add_fusion = f32[384,32,128]{2,0,1:T(8,128)S(1)} fusion(f32[384,32,128]{2,0,1:T(8,128)S(1)} %bitcast.44, f32[384,32]{0,1:T(8,128)S(1)} %get-tuple-element.230, f32[32,256,384]{2,1,0:T(8,128)S(1)} %get-tuple-element.239, f32[384,32]{0,1:T(8,128)S(1)} %max.8, f32[384,256]{0,1:T(8,128)S(1)} %subtract_convert_fusion, f32[32]{0:T(128)S(1)} %get-tuple-element.141, ...), kind=kOutput, calls=%fused_computation.6 | convolution fusion | flops 830472192 | bytes 27853440 | tf_op jit(solution)/shard_map/while/body/eval_jaxpr/cond/branch_1_fun/qhk,khd->qhd/dot_general | solution.py:47
  169.1 2.7 copy-done
  171.7 2.5 fusion.25
  174.2 1.9 collective-permute-start.4
  176.1 3.4 %collective-permute-start.7 = (f32[128,32,128]{2,0,1:T(8,128)S(1)}, f32[128,32,128]{2,0,1:T(8,128)S(1)}, u32[]{:S(2)}, u32[]{:S(2)}) collective-permute-start(f32[128,32,128]{2,0,1:T(8,128)S(1)} %get-tuple-element.243), channel_id=1, source_target_pairs={{0,8},{4,12},{8,16},{12,20},{16,24},{20,28},{24,32},{28,36},{32,40... | collective-permute-start | bytes 6291464 | tf_op jit(solution)/shard_map/ppermute | solution.py:14
  179.6 3.2 %collective-permute-start.2 = (f32[128,32]{0,1:T(8,128)S(1)}, f32[128,32]{0,1:T(8,128)S(1)}, u32[]{:S(2)}, u32[]{:S(2)}) collective-permute-start(f32[128,32]{0,1:T(8,128)S(1)} %get-tuple-element.246), channel_id=1, source_target_pairs={{0,4},{4,8},{8,12},{12,16},{16,20},{20,24},{24,28},{28,32},{32,36}... | collective-permute-start | bytes 49160 | tf_op jit(solution)/shard_map/ppermute | solution.py:14
  182.8 2.2 collective-permute-start.3
  185.0 3.4 %collective-permute-start.5 = (f32[128,32]{0,1:T(8,128)S(1)}, f32[128,32]{0,1:T(8,128)S(1)}, u32[]{:S(2)}, u32[]{:S(2)}) collective-permute-start(f32[128,32]{0,1:T(8,128)S(1)} %get-tuple-element.247), channel_id=1, source_target_pairs={{0,8},{4,12},{8,16},{12,20},{16,24},{20,28},{24,32},{28,36},{32,40... | collective-permute-start | bytes 49160 | tf_op jit(solution)/shard_map/ppermute | solution.py:14
  188.4 61.8 %collective-permute-done.2 = f32[128,32]{0,1:T(8,128)S(1)} collective-permute-done((f32[128,32]{0,1:T(8,128)S(1)}, f32[128,32]{0,1:T(8,128)S(1)}, u32[]{:S(2)}, u32[]{:S(2)}) %collective-permute-start.2) | collective-permute-done | bytes 16416 | tf_op jit(solution)/shard_map/ppermute | solution.py:14
  250.2 1.9 collective-permute-start.6
  252.1 7.0 %collective-permute-done.6 = f32[128,32]{0,1:T(8,128)S(1)} collective-permute-done((f32[128,32]{0,1:T(8,128)S(1)}, f32[128,32]{0,1:T(8,128)S(1)}, u32[]{:S(2)}, u32[]{:S(2)}) %collective-permute-start.6) | collective-permute-done | bytes 16416 | tf_op jit(solution)/shard_map/ppermute | solution.py:14
  259.2 7.0 %copy_bitcast_fusion = bf16[128,4096]{1,0:T(8,128)(2,1)} fusion(f32[128,32]{0,1:T(8,128)S(1)} %get-tuple-element.233, f32[128,32,128]{2,0,1:T(8,128)S(1)} %collective-permute-done.7, f32[128,32]{0,1:T(8,128)S(1)} %get-tuple-element.237, f32[128,32]{0,1:T(8,128)S(1)} %get-tuple-element.236, f32[128,32,128]{2,0,1:T(8,128)S(1)} %collective-permute-done.4, ...), kind=kLoop, calls=%fused_computation.27 | loop fusion | flops 4194304 | bytes 7421952 | tf_op jit(solution)/shard_map/reshape | solution.py:164
  (47 shorter events, 0.3 us)
Async XLA Ops:
  6.5 5.1 %copy-start.3 = (bf16[128,4096]{1,0:T(8,128)(2,1)S(1)}, bf16[128,4096]{1,0:T(8,128)(2,1)}, u32[]{:S(2)}) copy-start(bf16[128,4096]{1,0:T(8,128)(2,1)} %param.9) | copy-start | bytes 3145732
  6.5 12.9 %copy-start.6 = (s32[128]{0:T(128)S(1)}, s32[128]{0:T(128)}, u32[]{:S(2)}) copy-start(s32[128]{0:T(128)} %param.12) | copy-start | bytes 1540
  6.5 58.3 %all-gather.3.cloned.1.call-start = ((), (), s32[]{:S(2)}) async-start(), calls=%async_computation | async-start | bytes 5242880 | tf_op jit(solution)/shard_map/all_gather | solution.py:152
  9.1 111.9 %all-gather.5.cloned.1.call-start = ((), (), s32[]{:S(2)}) async-start(), calls=%async_computation.1 | async-start | bytes 5242880 | tf_op jit(solution)/shard_map/all_gather | solution.py:155
  12.3 25.4 %copy-start.1 = (bf16[128,4096]{0,1:T(8,128)(2,1)}, bf16[128,4096]{0,1:T(8,128)(2,1)S(1)}, u32[]{:S(2)}) copy-start(bf16[128,4096]{0,1:T(8,128)(2,1)S(1)} %copy.25) | copy-start | bytes 3145732
  12.3 25.4 %collective-permute-start = (bf16[128,32,128]{0,2,1:T(8,128)(2,1)S(1)}, bf16[128,32,128]{0,2,1:T(8,128)(2,1)S(1)}, u32[]{:S(2)}, u32[]{:S(2)}) collective-permute-start(bf16[128,32,128]{0,2,1:T(8,128)(2,1)S(1)} %bitcast.49), channel_id=1, source_target_pairs={{4,0},{8,4},{12,8},{16,12},{20,16},{24,20},{28,24},{32,28},{36,32}... | collective-permute-start | bytes 3145736 | tf_op jit(solution)/shard_map/ppermute | solution.py:14
  16.2 34.9 %collective-permute-start.1 = (bf16[128,32,128]{0,2,1:T(8,128)(2,1)S(1)}, bf16[128,32,128]{0,2,1:T(8,128)(2,1)}, u32[]{:S(2)}, u32[]{:S(2)}) collective-permute-start(bf16[128,32,128]{0,2,1:T(8,128)(2,1)S(1)} %bitcast.50), channel_id=1, source_target_pairs={{8,0},{12,4},{16,8},{20,12},{24,16},{28,20},{32,24},{36,28},{40,32... | collective-permute-start | bytes 3145736 | tf_op jit(solution)/shard_map/ppermute | solution.py:14
  37.6 1.0 copy-start.4
  121.0 9.4 %copy-start.2 = (bf16[384,32,128]{2,0,1:T(8,128)(2,1)S(1)}, bf16[384,32,128]{2,0,1:T(8,128)(2,1)}, u32[]{:S(2)}) copy-start(bf16[384,32,128]{2,0,1:T(8,128)(2,1)} %copy.27) | copy-start | bytes 9437188
  121.0 9.4 %copy-start.5 = (f32[32]{0:T(128)S(1)}, f32[32]{0:T(128)}, u32[]{:S(2)}) copy-start(f32[32]{0:T(128)} %param.13) | copy-start | bytes 388
  131.9 9.0 %slice-start = ((s8[6291456]{0:T(1024)(128)(4,1)}), s8[4194304]{0:T(1024)(128)(4,1)S(1)}, s32[]{:S(2)}) async-start(s8[6291456]{0:T(1024)(128)(4,1)} %bitcast.43), calls=%async_computation.2 | async-start | bytes 8388608 | tf_op jit(solution)/shard_map/while/body/eval_jaxpr/cond
  132.0 8.9 %slice-start.1 = ((s8[6291456]{0:T(1024)(128)(4,1)}), s8[2097152]{0:T(1024)(128)(4,1)S(1)}, s32[]{:S(2)}) async-start(s8[6291456]{0:T(1024)(128)(4,1)} %bitcast.43), calls=%async_computation.3 | async-start | bytes 4194304 | tf_op jit(solution)/shard_map/while/body/eval_jaxpr/cond
  148.4 2.7 copy-start
  152.5 9.0 %slice-start = ((s8[6291456]{0:T(1024)(128)(4,1)}), s8[4194304]{0:T(1024)(128)(4,1)S(1)}, s32[]{:S(2)}) async-start(s8[6291456]{0:T(1024)(128)(4,1)} %bitcast.43), calls=%async_computation.2 | async-start | bytes 8388608 | tf_op jit(solution)/shard_map/while/body/eval_jaxpr/cond
  152.7 8.9 %slice-start.1 = ((s8[6291456]{0:T(1024)(128)(4,1)}), s8[2097152]{0:T(1024)(128)(4,1)S(1)}, s32[]{:S(2)}) async-start(s8[6291456]{0:T(1024)(128)(4,1)} %bitcast.43), calls=%async_computation.3 | async-start | bytes 4194304 | tf_op jit(solution)/shard_map/while/body/eval_jaxpr/cond
  169.0 2.7 copy-start
  174.2 84.9 %collective-permute-start.4 = (f32[128,32,128]{2,0,1:T(8,128)S(1)}, f32[128,32,128]{2,0,1:T(8,128)S(1)}, u32[]{:S(2)}, u32[]{:S(2)}) collective-permute-start(f32[128,32,128]{2,0,1:T(8,128)S(1)} %get-tuple-element.242), channel_id=1, source_target_pairs={{0,4},{4,8},{8,12},{12,16},{16,20},{20,24},{24,28},{28,32},{32,36}... | collective-permute-start | bytes 6291464 | tf_op jit(solution)/shard_map/ppermute | solution.py:14
  176.1 83.0 %collective-permute-start.7 = (f32[128,32,128]{2,0,1:T(8,128)S(1)}, f32[128,32,128]{2,0,1:T(8,128)S(1)}, u32[]{:S(2)}, u32[]{:S(2)}) collective-permute-start(f32[128,32,128]{2,0,1:T(8,128)S(1)} %get-tuple-element.243), channel_id=1, source_target_pairs={{0,8},{4,12},{8,16},{12,20},{16,24},{20,28},{24,32},{28,36},{32,40... | collective-permute-start | bytes 6291464 | tf_op jit(solution)/shard_map/ppermute | solution.py:14
  179.6 70.6 %collective-permute-start.2 = (f32[128,32]{0,1:T(8,128)S(1)}, f32[128,32]{0,1:T(8,128)S(1)}, u32[]{:S(2)}, u32[]{:S(2)}) collective-permute-start(f32[128,32]{0,1:T(8,128)S(1)} %get-tuple-element.246), channel_id=1, source_target_pairs={{0,4},{4,8},{8,12},{12,16},{16,20},{20,24},{24,28},{28,32},{32,36}... | collective-permute-start | bytes 49160 | tf_op jit(solution)/shard_map/ppermute | solution.py:14
  182.8 69.3 %collective-permute-start.3 = (f32[128,32]{0,1:T(8,128)S(1)}, f32[128,32]{0,1:T(8,128)S(1)}, u32[]{:S(2)}, u32[]{:S(2)}) collective-permute-start(f32[128,32]{0,1:T(8,128)S(1)} %get-tuple-element.245), channel_id=1, source_target_pairs={{0,4},{4,8},{8,12},{12,16},{16,20},{20,24},{24,28},{28,32},{32,36}... | collective-permute-start | bytes 49160 | tf_op jit(solution)/shard_map/ppermute | solution.py:14
  185.0 67.1 %collective-permute-start.5 = (f32[128,32]{0,1:T(8,128)S(1)}, f32[128,32]{0,1:T(8,128)S(1)}, u32[]{:S(2)}, u32[]{:S(2)}) collective-permute-start(f32[128,32]{0,1:T(8,128)S(1)} %get-tuple-element.247), channel_id=1, source_target_pairs={{0,8},{4,12},{8,16},{12,20},{16,24},{20,28},{24,32},{28,36},{32,40... | collective-permute-start | bytes 49160 | tf_op jit(solution)/shard_map/ppermute | solution.py:14
  250.2 8.9 %collective-permute-start.6 = (f32[128,32]{0,1:T(8,128)S(1)}, f32[128,32]{0,1:T(8,128)S(1)}, u32[]{:S(2)}, u32[]{:S(2)}) collective-permute-start(f32[128,32]{0,1:T(8,128)S(1)} %get-tuple-element.244), channel_id=1, source_target_pairs={{0,8},{4,12},{8,16},{12,20},{16,24},{20,28},{24,32},{28,36},{32,40... | collective-permute-start | bytes 49160 | tf_op jit(solution)/shard_map/ppermute | solution.py:14
Sparse Core Ops, SparseCore 0:
  9.5 55.3 all-gather.2
  66.9 53.9 all-gather.4
where the time goes:
time: 274 us; the launch traced here: 273 us
  waiting for transfers between devices  157 us (57%)
  local copies, waits for them, and re-layouts  32.9 us (12%)
  matrix products  24 us (9%)
  starting transfers between devices  23.2 us (8%)
  other arithmetic  20.6 us (8%)
  between operations  13.6 us (5%)
    ppermute x8, waiting for transfers between devices, shifted(): lax.ppermute(value, axis, [(source, source + steps) for source in range(f...  98.4 us
    all_gather x1, waiting for transfers between devices, per_device(): lax.all_gather(value_states.reshape(rows_dev, head_count, head_width), 'i...  50.3 us
    ppermute x8, starting transfers between devices, shifted(): lax.ppermute(value, axis, [(source, source + steps) for source in range(f...  23.2 us
    dot_general x2, matrix products, update(): jnp.einsum('qhk,khd->qhd', weights.astype(jnp.bfloat16), value_slab, pref...  15 us
    while x3, local copies, waits for them, and re-layouts, attend_keys(): result, unused = lax.scan(scan_step, status, stacked)  14.8 us
    dot_general x2, matrix products, update(): jnp.einsum('qhd,khd->qhk', query_rows, key_slab, preferred_element_type=j...  9.01 us
    reduce_sum x2, other arithmetic, update(): row_total = row_total * rescale + jnp.sum(weights, axis=-1)  8.57 us
    all_gather x1, waiting for transfers between devices, per_device(): lax.all_gather(key_states.reshape(rows_dev, head_count, head_width), 'inn...  8.4 us
  transfers between devices with their start and end apart: 10, of which 6 were waited for; matrix products, arithmetic and copies ran while one was open for 6% of the time, Pallas kernels for 0%

commit v1 on v0

--- a/solution.py
+++ b/solution.py
@@ -1,3 +1,4 @@
+import functools
 import math
 import jax
 import jax.numpy as jnp
@@ -6,6 +7,38 @@
 
 SPAN = 2
 NEG_FILL = -1e30
+
+
+def touch_spot(row_data, shard_axis):
+    before = lax.axis_size(shard_axis)
+    ready, finding, shaped = (before, lax.axis_index(shard_axis), row_data.shape[0])
+    frames = []
+    for c, idx in enumerate(row_data.shape):
+        frames.append(idx * ready if c == 0 else idx)
+    next_value = lax.dynamic_update_slice_in_dim(
+        jnp.zeros(frames, row_data.dtype), row_data, finding * shaped, axis=0
+    )
+    now = far_arr = row_data
+    for no in [*range(1, ready // 2 + 1)]:
+        pile = []
+        for c in [*range(ready)]:
+            pile.append((c, (c + 1) % ready))
+        now = lax.ppermute(now, shard_axis, pile)
+        next_value = lax.dynamic_update_slice_in_dim(
+            next_value, now, (finding - no) % ready * shaped, axis=0
+        )
+        if 2 * no < ready:
+            vals = []
+            for c in tuple(range(ready)):
+                vals.append((c, (c - 1) % ready))
+            far_arr = lax.ppermute(far_arr, shard_axis, vals)
+            next_value = lax.dynamic_update_slice_in_dim(
+                next_value, far_arr, (finding + no) % ready * shaped, axis=0
+            )
+    return next_value
+
+
+balance_strips_all_now = functools.partial(touch_spot, shard_axis="inner")
 
 
 def shifted(value, axis, steps):
@@ -152,9 +185,7 @@
         lax.all_gather(
             key_states.reshape(rows_dev, head_count, head_width), "inner", axis=0, tiled=True
         ),
-        lax.all_gather(
-            value_states.reshape(rows_dev, head_count, head_width), "inner", axis=0, tiled=True
-        ),
+        balance_strips_all_now(value_states.reshape(rows_dev, head_count, head_width)),
     )
     key_pos = group_start + jnp.arange(portions[0].shape[0], dtype=jnp.int32)
     status = attend_keys(

time: 274 us -> 255 us (0.931)
  waiting for transfers between devices: 157 us -> 116 us
  local copies, waits for them, and re-layouts: 32.9 us -> 45.7 us
  starting transfers between devices: 23.2 us -> 33.4 us
    all_gather x1 -> x0, waiting for transfers between devices: 50.3 us -> none  [per_device(): lax.all_gather(value_states.reshape(rows_dev, head_count, head_width), 'i...]
    ppermute x0 -> x3, waiting for transfers between devices: none -> 48.8 us  [the longest x2 43.4 us: touch_spot(): now = lax.ppermute(now, shard_axis, pile)]
    ppermute x8, waiting for transfers between devices: 98.4 us -> 66.8 us  [shifted(): lax.ppermute(value, axis, [(source, source + steps) for source in range(f...]
    ppermute x0 -> x3, starting transfers between devices: none -> 10.2 us  [the longest x2 6.51 us: touch_spot(): now = lax.ppermute(now, shard_axis, pile)]
    dynamic_update_slice x0 -> x4, local copies, waits for them, and re-layouts: none -> 9.18 us  [the longest x2 4.59 us: touch_spot(): lax.dynamic_update_slice_in_dim(next_value, now, (finding - no) % ready *...]
    all_gather x1, waiting for transfers between devices: 8.4 us -> 0.01 us  [per_device(): lax.all_gather(key_states.reshape(rows_dev, head_count, head_width), 'inn...]
    unnamed x15 -> x13, local copies, waits for them, and re-layouts: 6.67 us -> 7.52 us
  transfers between devices with their start and end apart: 10 -> 12, of which waited for: 6 -> 5; matrix products, arithmetic and copies ran while one was open for 6% -> 11% of each run, Pallas kernels for 0% -> 0%
where the time goes in v1:
time: 255 us; the launch traced here: 254 us
  waiting for transfers between devices  116 us (45%)
  local copies, waits for them, and re-layouts  45.7 us (18%)
  starting transfers between devices  33.4 us (13%)
  matrix products  24 us (9%)
  other arithmetic  20.6 us (8%)
  between operations  13.7 us (5%)
    ppermute x8, waiting for transfers between devices, shifted(): lax.ppermute(value, axis, [(source, source + steps) for source in range(f...  66.8 us
    ppermute x2, waiting for transfers between devices, touch_spot(): now = lax.ppermute(now, shard_axis, pile)  43.4 us
    ppermute x8, starting transfers between devices, shifted(): lax.ppermute(value, axis, [(source, source + steps) for source in range(f...  23.2 us
    dot_general x2, matrix products, update(): jnp.einsum('qhk,khd->qhd', weights.astype(jnp.bfloat16), value_slab, pref...  15 us
    while x3, local copies, waits for them, and re-layouts, attend_keys(): result, unused = lax.scan(scan_step, status, stacked)  14.9 us
    dot_general x2, matrix products, update(): jnp.einsum('qhd,khd->qhk', query_rows, key_slab, preferred_element_type=j...  9.02 us
    reduce_sum x2, other arithmetic, update(): row_total = row_total * rescale + jnp.sum(weights, axis=-1)  8.57 us
    unnamed x13, local copies, waits for them, and re-layouts  7.52 us
  transfers between devices with their start and end apart: 12, of which 5 were waited for; matrix products, arithmetic and copies ran while one was open for 11% of the time, Pallas kernels for 0%

profile of v1, /device:TPU:256, one launch (start us, length us, event | category | flops | bytes accessed | tf_op | source)
XLA Modules:
  0.0 254.5 jit_solution(5811066365782132320)
XLA Ops:
  6.5 2.4 copy.32
  9.0 2.5 copy.33
  11.5 3.4 %collective-permute-start.2 = (bf16[128,32,128]{2,1,0:T(8,128)(2,1)}, bf16[128,32,128]{2,1,0:T(8,128)(2,1)}, u32[]{:S(2)}, u32[]{:S(2)}) collective-permute-start(bf16[128,32,128]{2,1,0:T(8,128)(2,1)} %bitcast.15), channel_id=1, source_target_pairs={{0,1},{1,2},{2,3},{3,0},{4,5},{5,6},{6,7},{7,4},{8,9},{9,10},{10,1... | collective-permute-start | bytes 3145736 | tf_op jit(solution)/shard_map/ppermute | solution.py:26
  14.9 1.6 copy.25
  16.5 3.6 %collective-permute-start = (bf16[128,32,128]{0,2,1:T(8,128)(2,1)S(1)}, bf16[128,32,128]{0,2,1:T(8,128)(2,1)S(1)}, u32[]{:S(2)}, u32[]{:S(2)}) collective-permute-start(bf16[128,32,128]{0,2,1:T(8,128)(2,1)S(1)} %bitcast.47), channel_id=1, source_target_pairs={{4,0},{8,4},{12,8},{16,12},{20,16},{24,20},{28,24},{32,28},{36,32}... | collective-permute-start | bytes 3145736 | tf_op jit(solution)/shard_map/ppermute | solution.py:47
  20.1 3.3 %collective-permute-start.1 = (bf16[128,32,128]{0,2,1:T(8,128)(2,1)S(1)}, bf16[128,32,128]{0,2,1:T(8,128)(2,1)}, u32[]{:S(2)}, u32[]{:S(2)}) collective-permute-start(bf16[128,32,128]{0,2,1:T(8,128)(2,1)S(1)} %bitcast.48), channel_id=1, source_target_pairs={{8,0},{12,4},{16,8},{20,12},{24,16},{28,20},{32,24},{36,28},{40,32... | collective-permute-start | bytes 3145736 | tf_op jit(solution)/shard_map/ppermute | solution.py:47
  23.4 3.7 %collective-permute-start.3 = (bf16[128,32,128]{2,1,0:T(8,128)(2,1)}, bf16[128,32,128]{2,1,0:T(8,128)(2,1)}, u32[]{:S(2)}, u32[]{:S(2)}) collective-permute-start(bf16[128,32,128]{2,1,0:T(8,128)(2,1)} %bitcast.15), channel_id=1, source_target_pairs={{0,3},{1,0},{2,1},{3,2},{4,7},{5,4},{6,5},{7,6},{8,11},{9,8},{10,9... | collective-permute-start | bytes 3145736 | tf_op jit(solution)/shard_map/ppermute | solution.py:34
  27.2 0.2 reduce-window.8
  27.5 0.2 convert_reduce_fusion
  27.8 21.9 %collective-permute-done.2 = bf16[128,32,128]{2,1,0:T(8,128)(2,1)} collective-permute-done((bf16[128,32,128]{2,1,0:T(8,128)(2,1)}, bf16[128,32,128]{2,1,0:T(8,128)(2,1)}, u32[]{:S(2)}, u32[]{:S(2)}) %collective-permute-start.2) | collective-permute-done | bytes 1048608 | tf_op jit(solution)/shard_map/ppermute | solution.py:26
  49.7 3.1 %collective-permute-start.4 = (bf16[128,32,128]{2,1,0:T(8,128)(2,1)}, bf16[128,32,128]{2,1,0:T(8,128)(2,1)}, u32[]{:S(2)}, u32[]{:S(2)}) collective-permute-start(bf16[128,32,128]{2,1,0:T(8,128)(2,1)} %collective-permute-done.2), channel_id=1, source_target_pairs={{0,1},{1,2},{2,3},{3,0},{4,5},{5,6},{6,7},{7,4},{8,9},{9,10},{10,1... | collective-permute-start | bytes 3145736 | tf_op jit(solution)/shard_map/ppermute | solution.py:26
  52.9 0.2 convert_reduce_fusion.1
  53.1 2.6 %broadcast_in_dim.65 = bf16[512,32,128]{2,1,0:T(8,128)(2,1)} broadcast(bf16[]{:T(256)} %constant.83.clone.1), dimensions={} | broadcast | bytes 4194306 | tf_op jit(solution)/shard_map/broadcast_in_dim | solution.py:19
  55.7 2.3 constant_dynamic-update-slice_fusion.3
  58.0 1.0 copy-done.3
  59.0 2.4 pad_maximum_fusion
  61.4 3.1 %copy.27 = bf16[384,32,128]{2,0,1:T(8,128)(2,1)} copy(bf16[384,32,128]{0,2,1:T(8,128)(2,1)S(1)} %pad_maximum_fusion) | data formatting | bytes 6291456 | tf_op jit(solution)/shard_map/while | solution.py:115
  64.5 2.3 constant_dynamic-update-slice_fusion.2
  66.7 5.4 %collective-permute-done.3 = bf16[128,32,128]{2,1,0:T(8,128)(2,1)} collective-permute-done((bf16[128,32,128]{2,1,0:T(8,128)(2,1)}, bf16[128,32,128]{2,1,0:T(8,128)(2,1)}, u32[]{:S(2)}, u32[]{:S(2)}) %collective-permute-start.3) | collective-permute-done | bytes 1048608 | tf_op jit(solution)/shard_map/ppermute | solution.py:34
  72.1 2.3 constant_dynamic-update-slice_fusion.1
  74.4 21.5 %collective-permute-done.4 = bf16[128,32,128]{2,1,0:T(8,128)(2,1)} collective-permute-done((bf16[128,32,128]{2,1,0:T(8,128)(2,1)}, bf16[128,32,128]{2,1,0:T(8,128)(2,1)}, u32[]{:S(2)}, u32[]{:S(2)}) %collective-permute-start.4) | collective-permute-done | bytes 1048608 | tf_op jit(solution)/shard_map/ppermute | solution.py:26
  96.0 2.3 constant_dynamic-update-slice_fusion
  98.3 5.8 %copy.28 = bf16[2,256,32,128]{3,1,2,0:T(8,128)(2,1)} copy(bf16[2,256,32,128]{3,2,1,0:T(8,128)(2,1)} %bitcast.9) | data formatting | bytes 8388608 | tf_op jit(solution)/shard_map/while | solution.py:115
  104.1 6.0 %copy.26 = bf16[2,256,32,128]{3,1,2,0:T(8,128)(2,1)} copy(bf16[2,256,32,128]{3,2,1,0:T(8,128)(2,1)} %bitcast.45) | data formatting | bytes 8388608 | tf_op jit(solution)/shard_map/while | solution.py:115
  110.1 3.4 %broadcast_in_dim.64 = f32[384,32,128]{2,0,1:T(8,128)} broadcast(f32[]{:T(128)} %constant.82.clone.1), dimensions={} | broadcast | bytes 6291460 | tf_op jit(solution)/shard_map/broadcast_in_dim | solution.py:59
  113.6 41.3 %while.14 = (s32[]{:T(128)}, f32[384,32]{0,1:T(8,128)S(1)}, f32[384,32]{0,1:T(8,128)S(1)}, f32[384,32,128]{2,0,1:T(8,128)}, s32[384]{0:T(512)S(1)}, /*index=5*/s...) while((s32[]{:T(128)}, f32[384,32]{0,1:T(8,128)S(1)}, ...), condition=%wide.region_9.10_spmd, body=%wide.region_3.9_spmd.sunk | while | flops 1674141696 | bytes 104477920 | solution.py:115
  113.6 0.8 fusion.31
  115.1 19.2 %conditional.2 = ((f32[384,32]{0,1:T(8,128)S(1)}, f32[384,32]{0,1:T(8,128)S(1)}, f32[384,32,128]{2,0,1:T(8,128)})) conditional(s32[]{:T(128)} %convert_element_type.41, (f32[384,32]{0,1:T(8,128)S(1)}, f32[384,32]{0,1:T(8,128)S(1)}, f32[384,32,128]{2,0,1:T(8,128)}) %tuple.50, (pred[384,256]{0,1:T(8,128)(4,1)S(1)}, bf16[2,256,32,128]{3,1,2,0:T(8,128)(2,1)}, ...), branch_computations={%region_5.5_spmd, %region_6.8_spmd} | conditional | flops 1673748480 | bytes 104370152 | solution.py:92
  115.2 4.5 %fusion.3 = (f32[384,32]{0,1:T(8,128)S(1)}, f32[32,256,384]{2,1,0:T(8,128)S(1)}) fusion(f32[384,256]{0,1:T(8,128)S(1)} %subtract_convert_fusion, f32[32]{0:T(128)S(1)} %get-tuple-element.141, pred[384,256]{0,1:T(8,128)(4,1)S(1)} %get-tuple-element.137, bf16[384,32,128]{2,0,1:T(8,128)(2,1)S(1)} %get-tuple-element.140, ...), kind=kOutput, calls=%fused_computation.5 | convolution fusion | flops 821022720 | bytes 18367104 | tf_op jit(solution)/shard_map/while/body/eval_jaxpr/cond/branch_1_fun/qhd,khd->qhk/dot_general | solution.py:69
  119.7 4.3 %fusion.2 = f32[384,32]{0,1:T(8,128)S(1)} fusion(f32[32,256,384]{2,1,0:T(8,128)S(1)} %get-tuple-element.239, f32[384,32]{0,1:T(8,128)S(1)} %max.8, f32[384,256]{0,1:T(8,128)S(1)} %subtract_convert_fusion, f32[32]{0:T(128)S(1)} %get-tuple-element.141, pred[384,256]{0,1:T(8,128)(4,1)S(1)} %get-tuple-element.137), kind=kLoop, calls=%fused_computation.4 | loop fusion | flops 22007808 | bytes 13172864 | tf_op jit(solution)/shard_map/while/body/eval_jaxpr/cond/branch_1_fun/reduce_sum | solution.py:79
  124.1 7.5 %bitcast_add_fusion = f32[384,32,128]{2,0,1:T(8,128)S(1)} fusion(f32[384,32,128]{2,0,1:T(8,128)S(1)} %bitcast.44, f32[384,32]{0,1:T(8,128)S(1)} %get-tuple-element.230, f32[32,256,384]{2,1,0:T(8,128)S(1)} %get-tuple-element.239, f32[384,32]{0,1:T(8,128)S(1)} %max.8, f32[384,256]{0,1:T(8,128)S(1)} %subtract_convert_fusion, f32[32]{0:T(128)S(1)} %get-tuple-element.141, ...), kind=kOutput, calls=%fused_computation.6 | convolution fusion | flops 830472192 | bytes 27853440 | tf_op jit(solution)/shard_map/while/body/eval_jaxpr/cond/branch_1_fun/qhk,khd->qhd/dot_general | solution.py:80
  131.6 2.7 %copy-done = f32[384,32,128]{2,0,1:T(8,128)} copy-done((f32[384,32,128]{2,0,1:T(8,128)}, f32[384,32,128]{2,0,1:T(8,128)S(1)}, u32[]{:S(2)}) %copy-start) | copy-done | bytes 6291480 | tf_op jit(solution)/shard_map/while/body/eval_jaxpr/cond
  134.3 0.8 fusion.31
  135.7 19.2 %conditional.2 = ((f32[384,32]{0,1:T(8,128)S(1)}, f32[384,32]{0,1:T(8,128)S(1)}, f32[384,32,128]{2,0,1:T(8,128)})) conditional(s32[]{:T(128)} %convert_element_type.41, (f32[384,32]{0,1:T(8,128)S(1)}, f32[384,32]{0,1:T(8,128)S(1)}, f32[384,32,128]{2,0,1:T(8,128)}) %tuple.50, (pred[384,256]{0,1:T(8,128)(4,1)S(1)}, bf16[2,256,32,128]{3,1,2,0:T(8,128)(2,1)}, ...), branch_computations={%region_5.5_spmd, %region_6.8_spmd} | conditional | flops 1673748480 | bytes 104370152 | solution.py:92
  135.9 4.5 %fusion.3 = (f32[384,32]{0,1:T(8,128)S(1)}, f32[32,256,384]{2,1,0:T(8,128)S(1)}) fusion(f32[384,256]{0,1:T(8,128)S(1)} %subtract_convert_fusion, f32[32]{0:T(128)S(1)} %get-tuple-element.141, pred[384,256]{0,1:T(8,128)(4,1)S(1)} %get-tuple-element.137, bf16[384,32,128]{2,0,1:T(8,128)(2,1)S(1)} %get-tuple-element.140, ...), kind=kOutput, calls=%fused_computation.5 | convolution fusion | flops 821022720 | bytes 18367104 | tf_op jit(solution)/shard_map/while/body/eval_jaxpr/cond/branch_1_fun/qhd,khd->qhk/dot_general | solution.py:69
  140.4 4.3 %fusion.2 = f32[384,32]{0,1:T(8,128)S(1)} fusion(f32[32,256,384]{2,1,0:T(8,128)S(1)} %get-tuple-element.239, f32[384,32]{0,1:T(8,128)S(1)} %max.8, f32[384,256]{0,1:T(8,128)S(1)} %subtract_convert_fusion, f32[32]{0:T(128)S(1)} %get-tuple-element.141, pred[384,256]{0,1:T(8,128)(4,1)S(1)} %get-tuple-element.137), kind=kLoop, calls=%fused_computation.4 | loop fusion | flops 22007808 | bytes 13172864 | tf_op jit(solution)/shard_map/while/body/eval_jaxpr/cond/branch_1_fun/reduce_sum | solution.py:79
  144.8 7.5 %bitcast_add_fusion = f32[384,32,128]{2,0,1:T(8,128)S(1)} fusion(f32[384,32,128]{2,0,1:T(8,128)S(1)} %bitcast.44, f32[384,32]{0,1:T(8,128)S(1)} %get-tuple-element.230, f32[32,256,384]{2,1,0:T(8,128)S(1)} %get-tuple-element.239, f32[384,32]{0,1:T(8,128)S(1)} %max.8, f32[384,256]{0,1:T(8,128)S(1)} %subtract_convert_fusion, f32[32]{0:T(128)S(1)} %get-tuple-element.141, ...), kind=kOutput, calls=%fused_computation.6 | convolution fusion | flops 830472192 | bytes 27853440 | tf_op jit(solution)/shard_map/while/body/eval_jaxpr/cond/branch_1_fun/qhk,khd->qhd/dot_general | solution.py:80
  152.3 2.7 %copy-done = f32[384,32,128]{2,0,1:T(8,128)} copy-done((f32[384,32,128]{2,0,1:T(8,128)}, f32[384,32,128]{2,0,1:T(8,128)S(1)}, u32[]{:S(2)}) %copy-start) | copy-done | bytes 6291480 | tf_op jit(solution)/shard_map/while/body/eval_jaxpr/cond
  154.9 2.5 fusion.25
  157.4 3.5 %collective-permute-start.10 = (f32[128,32,128]{2,0,1:T(8,128)S(1)}, f32[128,32,128]{2,0,1:T(8,128)S(1)}, u32[]{:S(2)}, u32[]{:S(2)}) collective-permute-start(f32[128,32,128]{2,0,1:T(8,128)S(1)} %get-tuple-element.243), channel_id=1, source_target_pairs={{0,8},{4,12},{8,16},{12,20},{16,24},{20,28},{24,32},{28,36},{32,40... | collective-permute-start | bytes 6291464 | tf_op jit(solution)/shard_map/ppermute | solution.py:47
  160.9 1.9 collective-permute-start.7
  162.9 3.6 %collective-permute-start.5 = (f32[128,32]{0,1:T(8,128)S(1)}, f32[128,32]{0,1:T(8,128)S(1)}, u32[]{:S(2)}, u32[]{:S(2)}) collective-permute-start(f32[128,32]{0,1:T(8,128)S(1)} %get-tuple-element.246), channel_id=1, source_target_pairs={{0,4},{4,8},{8,12},{12,16},{16,20},{20,24},{24,28},{28,32},{32,36}... | collective-permute-start | bytes 49160 | tf_op jit(solution)/shard_map/ppermute | solution.py:47
  166.5 1.9 collective-permute-start.6
  168.4 3.5 %collective-permute-start.8 = (f32[128,32]{0,1:T(8,128)S(1)}, f32[128,32]{0,1:T(8,128)S(1)}, u32[]{:S(2)}, u32[]{:S(2)}) collective-permute-start(f32[128,32]{0,1:T(8,128)S(1)} %get-tuple-element.247), channel_id=1, source_target_pairs={{0,8},{4,12},{8,16},{12,20},{16,24},{20,28},{24,32},{28,36},{32,40... | collective-permute-start | bytes 49160 | tf_op jit(solution)/shard_map/ppermute | solution.py:47
  171.9 59.8 %collective-permute-done.5 = f32[128,32]{0,1:T(8,128)S(1)} collective-permute-done((f32[128,32]{0,1:T(8,128)S(1)}, f32[128,32]{0,1:T(8,128)S(1)}, u32[]{:S(2)}, u32[]{:S(2)}) %collective-permute-start.5) | collective-permute-done | bytes 16416 | tf_op jit(solution)/shard_map/ppermute | solution.py:47
  231.7 1.9 collective-permute-start.9
  233.6 7.0 %collective-permute-done.9 = f32[128,32]{0,1:T(8,128)S(1)} collective-permute-done((f32[128,32]{0,1:T(8,128)S(1)}, f32[128,32]{0,1:T(8,128)S(1)}, u32[]{:S(2)}, u32[]{:S(2)}) %collective-permute-start.9) | collective-permute-done | bytes 16416 | tf_op jit(solution)/shard_map/ppermute | solution.py:47
  240.7 7.0 %copy_bitcast_fusion = bf16[128,4096]{1,0:T(8,128)(2,1)} fusion(f32[128,32]{0,1:T(8,128)S(1)} %get-tuple-element.233, f32[128,32,128]{2,0,1:T(8,128)S(1)} %collective-permute-done.10, f32[128,32]{0,1:T(8,128)S(1)} %get-tuple-element.237, f32[128,32]{0,1:T(8,128)S(1)} %get-tuple-element.236, f32[128,32,128]{2,0,1:T(8,128)S(1)} %collective-permute-done.7, ...), kind=kLoop, calls=%fused_computation.27 | loop fusion | flops 4194304 | bytes 7421952 | tf_op jit(solution)/shard_map/reshape | solution.py:195
  (53 shorter events, 0.7 us)
Async XLA Ops:
  6.5 20.6 %copy-start.5 = (s32[128]{0:T(128)S(1)}, s32[128]{0:T(128)}, u32[]{:S(2)}) copy-start(s32[128]{0:T(128)} %param.12) | copy-start | bytes 1540
  6.5 97.6 %all-gather.2.cloned.1.call-start = ((), (), s32[]{:S(2)}) async-start(), calls=%async_computation | async-start | bytes 5242880 | tf_op jit(solution)/shard_map/all_gather | solution.py:185
  11.5 38.3 %collective-permute-start.2 = (bf16[128,32,128]{2,1,0:T(8,128)(2,1)}, bf16[128,32,128]{2,1,0:T(8,128)(2,1)}, u32[]{:S(2)}, u32[]{:S(2)}) collective-permute-start(bf16[128,32,128]{2,1,0:T(8,128)(2,1)} %bitcast.15), channel_id=1, source_target_pairs={{0,1},{1,2},{2,3},{3,0},{4,5},{5,6},{6,7},{7,4},{8,9},{9,10},{10,1... | collective-permute-start | bytes 3145736 | tf_op jit(solution)/shard_map/ppermute | solution.py:26
  16.5 41.5 %copy-start.1 = (bf16[128,4096]{0,1:T(8,128)(2,1)}, bf16[128,4096]{0,1:T(8,128)(2,1)S(1)}, u32[]{:S(2)}) copy-start(bf16[128,4096]{0,1:T(8,128)(2,1)S(1)} %copy.25) | copy-start | bytes 3145732
  16.5 41.5 %collective-permute-start = (bf16[128,32,128]{0,2,1:T(8,128)(2,1)S(1)}, bf16[128,32,128]{0,2,1:T(8,128)(2,1)S(1)}, u32[]{:S(2)}, u32[]{:S(2)}) collective-permute-start(bf16[128,32,128]{0,2,1:T(8,128)(2,1)S(1)} %bitcast.47), channel_id=1, source_target_pairs={{4,0},{8,4},{12,8},{16,12},{20,16},{24,20},{28,24},{32,28},{36,32}... | collective-permute-start | bytes 3145736 | tf_op jit(solution)/shard_map/ppermute | solution.py:47
  20.1 38.9 %collective-permute-start.1 = (bf16[128,32,128]{0,2,1:T(8,128)(2,1)S(1)}, bf16[128,32,128]{0,2,1:T(8,128)(2,1)}, u32[]{:S(2)}, u32[]{:S(2)}) collective-permute-start(bf16[128,32,128]{0,2,1:T(8,128)(2,1)S(1)} %bitcast.48), channel_id=1, source_target_pairs={{8,0},{12,4},{16,8},{20,12},{24,16},{28,20},{32,24},{36,28},{40,32... | collective-permute-start | bytes 3145736 | tf_op jit(solution)/shard_map/ppermute | solution.py:47
  23.4 48.7 %collective-permute-start.3 = (bf16[128,32,128]{2,1,0:T(8,128)(2,1)}, bf16[128,32,128]{2,1,0:T(8,128)(2,1)}, u32[]{:S(2)}, u32[]{:S(2)}) collective-permute-start(bf16[128,32,128]{2,1,0:T(8,128)(2,1)} %bitcast.15), channel_id=1, source_target_pairs={{0,3},{1,0},{2,1},{3,2},{4,7},{5,4},{6,5},{7,6},{8,11},{9,8},{10,9... | collective-permute-start | bytes 3145736 | tf_op jit(solution)/shard_map/ppermute | solution.py:34
  49.7 46.2 %collective-permute-start.4 = (bf16[128,32,128]{2,1,0:T(8,128)(2,1)}, bf16[128,32,128]{2,1,0:T(8,128)(2,1)}, u32[]{:S(2)}, u32[]{:S(2)}) collective-permute-start(bf16[128,32,128]{2,1,0:T(8,128)(2,1)} %collective-permute-done.2), channel_id=1, source_target_pairs={{0,1},{1,2},{2,3},{3,0},{4,5},{5,6},{6,7},{7,4},{8,9},{9,10},{10,1... | collective-permute-start | bytes 3145736 | tf_op jit(solution)/shard_map/ppermute | solution.py:26
  58.0 1.0 copy-start.3
  104.1 9.4 %copy-start.2 = (bf16[384,32,128]{2,0,1:T(8,128)(2,1)S(1)}, bf16[384,32,128]{2,0,1:T(8,128)(2,1)}, u32[]{:S(2)}) copy-start(bf16[384,32,128]{2,0,1:T(8,128)(2,1)} %copy.27) | copy-start | bytes 9437188
  104.1 9.4 %copy-start.4 = (f32[32]{0:T(128)S(1)}, f32[32]{0:T(128)}, u32[]{:S(2)}) copy-start(f32[32]{0:T(128)} %param.13) | copy-start | bytes 388
  115.1 9.0 %slice-start = ((s8[6291456]{0:T(1024)(128)(4,1)}), s8[4194304]{0:T(1024)(128)(4,1)S(1)}, s32[]{:S(2)}) async-start(s8[6291456]{0:T(1024)(128)(4,1)} %bitcast.43), calls=%async_computation.1 | async-start | bytes 8388608 | tf_op jit(solution)/shard_map/while/body/eval_jaxpr/cond
  115.2 8.9 %slice-start.1 = ((s8[6291456]{0:T(1024)(128)(4,1)}), s8[2097152]{0:T(1024)(128)(4,1)S(1)}, s32[]{:S(2)}) async-start(s8[6291456]{0:T(1024)(128)(4,1)} %bitcast.43), calls=%async_computation.2 | async-start | bytes 4194304 | tf_op jit(solution)/shard_map/while/body/eval_jaxpr/cond
  131.6 2.7 %copy-start = (f32[384,32,128]{2,0,1:T(8,128)}, f32[384,32,128]{2,0,1:T(8,128)S(1)}, u32[]{:S(2)}) copy-start(f32[384,32,128]{2,0,1:T(8,128)S(1)} %bitcast_add_fusion) | copy-start | bytes 18874372 | tf_op jit(solution)/shard_map/while/body/eval_jaxpr/cond
  135.7 9.0 %slice-start = ((s8[6291456]{0:T(1024)(128)(4,1)}), s8[4194304]{0:T(1024)(128)(4,1)S(1)}, s32[]{:S(2)}) async-start(s8[6291456]{0:T(1024)(128)(4,1)} %bitcast.43), calls=%async_computation.1 | async-start | bytes 8388608 | tf_op jit(solution)/shard_map/while/body/eval_jaxpr/cond
  135.8 8.9 %slice-start.1 = ((s8[6291456]{0:T(1024)(128)(4,1)}), s8[2097152]{0:T(1024)(128)(4,1)S(1)}, s32[]{:S(2)}) async-start(s8[6291456]{0:T(1024)(128)(4,1)} %bitcast.43), calls=%async_computation.2 | async-start | bytes 4194304 | tf_op jit(solution)/shard_map/while/body/eval_jaxpr/cond
  152.2 2.7 %copy-start = (f32[384,32,128]{2,0,1:T(8,128)}, f32[384,32,128]{2,0,1:T(8,128)S(1)}, u32[]{:S(2)}) copy-start(f32[384,32,128]{2,0,1:T(8,128)S(1)} %bitcast_add_fusion) | copy-start | bytes 18874372 | tf_op jit(solution)/shard_map/while/body/eval_jaxpr/cond
  157.4 83.2 %collective-permute-start.10 = (f32[128,32,128]{2,0,1:T(8,128)S(1)}, f32[128,32,128]{2,0,1:T(8,128)S(1)}, u32[]{:S(2)}, u32[]{:S(2)}) collective-permute-start(f32[128,32,128]{2,0,1:T(8,128)S(1)} %get-tuple-element.243), channel_id=1, source_target_pairs={{0,8},{4,12},{8,16},{12,20},{16,24},{20,28},{24,32},{28,36},{32,40... | collective-permute-start | bytes 6291464 | tf_op jit(solution)/shard_map/ppermute | solution.py:47
  160.9 79.7 %collective-permute-start.7 = (f32[128,32,128]{2,0,1:T(8,128)S(1)}, f32[128,32,128]{2,0,1:T(8,128)S(1)}, u32[]{:S(2)}, u32[]{:S(2)}) collective-permute-start(f32[128,32,128]{2,0,1:T(8,128)S(1)} %get-tuple-element.242), channel_id=1, source_target_pairs={{0,4},{4,8},{8,12},{12,16},{16,20},{20,24},{24,28},{28,32},{32,36}... | collective-permute-start | bytes 6291464 | tf_op jit(solution)/shard_map/ppermute | solution.py:47
  162.9 68.8 %collective-permute-start.5 = (f32[128,32]{0,1:T(8,128)S(1)}, f32[128,32]{0,1:T(8,128)S(1)}, u32[]{:S(2)}, u32[]{:S(2)}) collective-permute-start(f32[128,32]{0,1:T(8,128)S(1)} %get-tuple-element.246), channel_id=1, source_target_pairs={{0,4},{4,8},{8,12},{12,16},{16,20},{20,24},{24,28},{28,32},{32,36}... | collective-permute-start | bytes 49160 | tf_op jit(solution)/shard_map/ppermute | solution.py:47
  166.5 67.1 %collective-permute-start.6 = (f32[128,32]{0,1:T(8,128)S(1)}, f32[128,32]{0,1:T(8,128)S(1)}, u32[]{:S(2)}, u32[]{:S(2)}) collective-permute-start(f32[128,32]{0,1:T(8,128)S(1)} %get-tuple-element.245), channel_id=1, source_target_pairs={{0,4},{4,8},{8,12},{12,16},{16,20},{20,24},{24,28},{28,32},{32,36}... | collective-permute-start | bytes 49160 | tf_op jit(solution)/shard_map/ppermute | solution.py:47
  168.4 65.2 %collective-permute-start.8 = (f32[128,32]{0,1:T(8,128)S(1)}, f32[128,32]{0,1:T(8,128)S(1)}, u32[]{:S(2)}, u32[]{:S(2)}) collective-permute-start(f32[128,32]{0,1:T(8,128)S(1)} %get-tuple-element.247), channel_id=1, source_target_pairs={{0,8},{4,12},{8,16},{12,20},{16,24},{20,28},{24,32},{28,36},{32,40... | collective-permute-start | bytes 49160 | tf_op jit(solution)/shard_map/ppermute | solution.py:47
  231.7 8.9 %collective-permute-start.9 = (f32[128,32]{0,1:T(8,128)S(1)}, f32[128,32]{0,1:T(8,128)S(1)}, u32[]{:S(2)}, u32[]{:S(2)}) collective-permute-start(f32[128,32]{0,1:T(8,128)S(1)} %get-tuple-element.244), channel_id=1, source_target_pairs={{0,8},{4,12},{8,16},{12,20},{16,24},{20,28},{24,32},{28,36},{32,40... | collective-permute-start | bytes 49160 | tf_op jit(solution)/shard_map/ppermute | solution.py:47
Sparse Core Ops, SparseCore 0:
  9.5 83.9 all-gather.1
